TPU v7x, 32 devices: a whole 2x2x4 slice. The times are simulated.
32 devices in a mesh: groups: 2 (over y), dp: 8 (over z, x), tensor: 2 (over core).
Axes of the slice: x: 2, y: 2, z: 4, core: 2. Of those that a mesh axis runs over, the one named last changes fastest.
Arguments:
- xbc: bfloat16 [2048, 9216], P(('groups', 'dp', 'tensor')), parts along dimension 0, may hold values from -6 to 6
- gate_z: bfloat16 [2048, 8192], P(('groups', 'dp', 'tensor')), parts along dimension 0, may hold values from -6 to 6
- dt_raw: bfloat16 [2048, 128], P(('groups', 'dp', 'tensor')), parts along dimension 0, may hold values from -6 to 6
- conv_weight: float32 [4, 9216], replicated, may hold values from -3 to 3
- conv_bias: float32 [9216], replicated, may hold values from -3 to 3
- dt_bias: float32 [128], P('tensor'), may hold values from -4 to -1
- decay_rate: float32 [128], P('tensor'), may hold values from 0.02 to 2
- d_skip: float32 [128], P('tensor'), may hold values from 0.5 to 2
- norm_gain: float32 [8192], P('tensor'), may hold values from 0.5 to 1.5
- ssm_store: bfloat16 [16, 128, 64, 128], P(('groups', 'dp'), 'tensor'), parts along dimension 0, may hold values from -1.1953125 to 1.1953125
- conv_store: bfloat16 [16, 3, 9216], P(('groups', 'dp'), None, 'tensor'), parts along dimension 0, may hold values from -6 to 6
- source_of: int32 [16], P('groups'), parts along dimension 0, may hold values from 0 to 7, each once
- prefix_len: int32 [16], P(('groups', 'dp')), parts along dimension 0, may hold values from 0 to 8192, as said below
- span_len: int32 [16], P(('groups', 'dp')), parts along dimension 0, may hold values from 32 to 128
Outputs:
- mixed: bfloat16 [2048, 8192], P(('groups', 'dp'), 'tensor'), parts along dimension 0
There are 2 independent parts, one for each index of `groups`. A program takes and returns all parts, laid end to end along the dimension named above; an argument that names none is the same for every part. Nothing has to cross between parts.
Inputs may be any that keep to these rules, and one draw needn't show every extreme that they name: `source_of`: each of 0 to 7 appears once. `prefix_len`: 0 marks a request without kept states.
All inputs are finite; a program needn't handle non-finite values.
Results may differ from a plain program's by a relative error of at most 0.0045.
Values may be sent and summed in bfloat16 or wider, within the bound.
A program may use at most 64 MiB of HBM per device.

v0:
```python
import jax
import jax.numpy as jnp
from jax import lax
from jax.sharding import PartitionSpec as P

HEAD_DIM = 64
STATE = 128
NORM_WIDTH = 2048


EPSILON = 1e-05


def from_behind(value, axis, steps):
    count = lax.axis_size(axis)
    initial, last = (max(0, -steps), min(count, count - steps))
    return lax.ppermute(value, axis, [(source, source + steps) for source in range(initial, last)])


def convolve(rims, rows, weight, bias):
    extended = jnp.concatenate([rims, rows], axis=0).astype(jnp.float32)
    count = rows.shape[0]
    total = bias[None, :]
    for offset in range(weight.shape[0]):
        total = total + weight[offset][None, :] * extended[offset : offset + count]
    return jax.nn.silu(total).astype(jnp.bfloat16)


def regroup(payload):
    whole = (
        lax.all_gather(payload[0], "tensor", axis=0, tiled=True),
        lax.all_gather(payload[1], "tensor", axis=0, tiled=True),
        lax.all_gather(payload[2], "tensor", axis=0, tiled=True),
    )
    core = lax.axis_index("tensor")
    halves = lax.axis_size("tensor")
    kept = []
    for member in whole:
        width = member.shape[1] // halves
        kept.append(lax.dynamic_slice_in_dim(member, core * width, width, 1))
    return tuple(kept)


def migrate(ssm_store, conv_store, source_of):
    state_flat = ssm_store.reshape(1, -1)
    rims_flat = conv_store.reshape(1, -1)
    held_state, held_rims = (
        lax.all_to_all(state_flat, "dp", split_axis=1, concat_axis=0, tiled=True),
        lax.all_to_all(rims_flat, "dp", split_axis=1, concat_axis=0, tiled=True),
    )
    pick_state = jnp.take(held_state, source_of, axis=0)[:, None, :]
    pick_rims = jnp.take(held_rims, source_of, axis=0)[:, None, :]
    got_state, got_rims = (
        lax.all_to_all(pick_state, "dp", split_axis=0, concat_axis=1, tiled=True),
        lax.all_to_all(pick_rims, "dp", split_axis=0, concat_axis=1, tiled=True),
    )
    return (got_state.reshape(ssm_store.shape[1:]), got_rims.reshape(conv_store.shape[1:]))


def state_space(
    activated, gate_rows, dt_rows, dt_bias, decay_rate, d_skip, norm_gain, kept_state, live_rows
):
    count = activated.shape[0]
    heads = dt_bias.shape[0]
    inner = heads * HEAD_DIM
    groups = (activated.shape[1] - inner) // (2 * STATE)
    per_group = heads // groups
    x_heads = activated[:, :inner].reshape(count, heads, HEAD_DIM)
    b_proj = activated[:, inner : inner + groups * STATE].reshape(count, groups, STATE)
    c_proj = activated[:, inner + groups * STATE :].reshape(count, groups, STATE)
    step_size = jax.nn.softplus(dt_rows.astype(jnp.float32) + dt_bias[None, :])
    cumulative = jnp.cumsum(-decay_rate[None, :] * step_size, axis=0)
    scores = jnp.einsum("tgn,ugn->gtu", c_proj, b_proj, preferred_element_type=jnp.float32)
    spread = cumulative.T[:, :, None] - cumulative.T[:, None, :]
    causal = jnp.arange(count)[:, None] >= jnp.arange(count)[None, :]
    decay = jnp.where(causal, jnp.exp(jnp.where(causal, spread, 0.0)), 0.0)
    weights = (
        decay.reshape(groups, per_group, count, count)
        * scores[:, None]
        * step_size.T.reshape(groups, per_group, 1, count)
    )
    weights = weights.reshape(heads, count, count).astype(jnp.bfloat16)
    intra = jnp.einsum("htu,uhp->thp", weights, x_heads, preferred_element_type=jnp.float32)
    state_local = kept_state.reshape(groups, per_group, HEAD_DIM, STATE)
    carried = jnp.einsum("tgn,gkpn->tgkp", c_proj, state_local, preferred_element_type=jnp.float32)
    carried = carried.reshape(count, heads, HEAD_DIM) * jnp.exp(cumulative)[:, :, None]
    mixed = intra + carried + d_skip[None, :, None] * x_heads.astype(jnp.float32)
    gated = mixed.reshape(count, inner) * jax.nn.silu(gate_rows.astype(jnp.float32))
    grouped = gated.reshape(count, inner // NORM_WIDTH, NORM_WIDTH)
    scale = lax.rsqrt(jnp.mean(grouped * grouped, axis=-1, keepdims=True) + EPSILON)
    normed = (grouped * scale).reshape(count, inner) * norm_gain[None, :]
    return jnp.where(live_rows[:, None], normed, 0.0).astype(jnp.bfloat16)


def local(
    xbc,
    gate_z,
    dt_raw,
    conv_weight,
    conv_bias,
    dt_bias,
    decay_rate,
    d_skip,
    norm_gain,
    ssm_store,
    conv_store,
    source_of,
    prefix_len,
    span_len,
):
    kept_state, kept_rims = migrate(ssm_store, conv_store, source_of)
    live = prefix_len[0] > 0
    kept_state = jnp.where(live, kept_state, jnp.zeros_like(kept_state))
    kept_rims = jnp.where(live, kept_rims, jnp.zeros_like(kept_rims))
    core = lax.axis_index("tensor")
    full_rims = lax.all_gather(kept_rims, "tensor", axis=1, tiled=True)
    rim_count = conv_weight.shape[0] - 1
    before = from_behind(xbc[xbc.shape[0] - rim_count :], "tensor", 1)
    rims = jnp.where(core == 0, full_rims, before)
    activated_rows = convolve(rims, xbc, conv_weight, conv_bias)
    activated, gate_heads, dt_heads = regroup((activated_rows, gate_z, dt_raw))
    live_rows = jnp.arange(activated.shape[0]) < span_len[0]
    return state_space(
        activated,
        gate_heads,
        dt_heads,
        dt_bias,
        decay_rate,
        d_skip,
        norm_gain,
        kept_state,
        live_rows,
    )


def solution(mesh):
    in_specs = (
        P(("groups", "dp", "tensor"), None),
        P(("groups", "dp", "tensor"), None),
        P(("groups", "dp", "tensor"), None),
        P(),
        P(),
        P("tensor"),
        P("tensor"),
        P("tensor"),
        P("tensor"),
        P(("groups", "dp"), "tensor", None, None),
        P(("groups", "dp"), None, "tensor"),
        P("groups"),
        P(("groups", "dp")),
        P(("groups", "dp")),
    )
    out_specs = P(("groups", "dp"), "tensor")
    return jax.shard_map(local, mesh=mesh, in_specs=in_specs, out_specs=out_specs, check_vma=False)
```

profile of v0, /device:TPU:0, one launch (start us, length us, event | category | flops | bytes accessed | tf_op | source)
XLA Modules:
  0.0 140.2 jit_solution(3511456396031098447)
XLA Ops:
  6.5 1.0 all_to_all.46
  7.5 0.5 broadcast.127
  8.0 0.7 reduce.6
  8.7 0.7 reshape.176
  9.4 7.3 %all-to-all-start = ((bf16[8,2,864]{2,1,0:T(2,128)(2,1)}), bf16[8,2,864]{2,1,0:T(2,128)(2,1)S(1)}, u32[]{:S(2)}, u32[]{:S(2)}) async-start(bf16[8,2,864]{2,1,0:T(2,128)(2,1)} %reshape.176), calls=%async_computation | async-start | bytes 57344 | tf_op jit(solution)/shard_map/all_to_all | solution.py:49
  16.7 0.9 slice.37
  17.6 1.5 %collective-permute-start = (bf16[3,9216]{1,0:T(4,128)(2,1)S(1)}, bf16[3,9216]{1,0:T(4,128)(2,1)S(1)}, u32[]{:S(2)}, u32[]{:S(2)}) collective-permute-start(bf16[3,9216]{1,0:T(4,128)(2,1)S(1)} %slice.37), channel_id=1, source_target_pairs={{0,1},{2,3},{4,5},{6,7},{8,9},{10,11},{12,13},{14,15},{16,17},{18,... | collective-permute-start | bytes 165896 | tf_op jit(solution)/shard_map/ppermute | solution.py:17
  19.1 0.7 compare_select_fusion.1
  19.8 0.7 compare_and_fusion
  20.4 2.9 %all-to-all-done = bf16[8,2,864]{2,1,0:T(2,128)(2,1)S(1)} async-done(((bf16[8,2,864]{2,1,0:T(2,128)(2,1)}), bf16[8,2,864]{2,1,0:T(2,128)(2,1)S(1)}, u32[]{:S(2)}, u32[]{:S(2)}) %all-to-all-start) | async-done | bytes 27680 | tf_op jit(solution)/shard_map/all_to_all | solution.py:49
  23.5 0.6 gather_fusion
  24.1 0.6 reduce.7
  24.7 0.7 reshape.178
  25.4 3.3 %all-to-all-start.1 = ((bf16[8,2,864]{2,1,0:T(2,128)(2,1)}), bf16[8,2,864]{2,1,0:T(2,128)(2,1)S(1)}, u32[]{:S(2)}, u32[]{:S(2)}) async-start(bf16[8,2,864]{2,1,0:T(2,128)(2,1)} %reshape.178), calls=%async_computation.1 | async-start | bytes 57344 | tf_op jit(solution)/shard_map/all_to_all | solution.py:55
  28.8 1.3 fusion.17
  30.8 0.5 all_to_all.47
  31.3 6.9 %reduce.4 = bf16[8,65536]{1,0:T(8,128)(2,1)S(1)} reduce(bf16[8,1,65536]{2,1,0:T(2,128)(2,1)S(1)} %bitcast.62, bf16[]{:T(256)} %broadcast.127), dimensions={1}, to_apply=%bitcast.45.reduce_sub_computation | reduce | bytes 2097154
  38.2 1.9 %reshape.172 = bf16[8,2,32768]{2,1,0:T(2,128)(2,1)} reshape(bf16[8,65536]{1,0:T(8,128)(2,1)S(1)} %reduce.4) | data formatting | bytes 2097152
  40.1 5.9 %all-to-all-start.2 = ((bf16[8,2,32768]{2,1,0:T(2,128)(2,1)}), bf16[8,2,32768]{2,1,0:T(2,128)(2,1)S(1)}, u32[]{:S(2)}, u32[]{:S(2)}) async-start(bf16[8,2,32768]{2,1,0:T(2,128)(2,1)} %reshape.172), calls=%async_computation.2 | async-start | bytes 2097152 | tf_op jit(solution)/shard_map/all_to_all | solution.py:48
  46.4 2.0 %all_gather.12 = bf16[3,9216]{1,0:T(4,128)(2,1)S(1)} all-gather(bf16[3,4608]{1,0:T(4,128)(2,1)S(1)} %select_n.93), channel_id=1, replica_groups=mesh['groups'=2,'dp'=8,'tensor'=2] {'tensor'}, dimensions={1}, use_global_device_ids=true | all-gather | bytes 82944 | tf_op jit(solution)/shard_map/all_gather | solution.py:116
  49.2 2.5 %multiply_convert_fusion = bf16[64,9216]{1,0:T(8,128)(2,1)} fusion(f32[67,9216]{1,0:T(8,128)S(1)} %maximum_convert_fusion, f32[9216]{0:T(1024)S(1)} %bitcast.74, f32[9216]{0:T(1024)S(1)} %bitcast.75, f32[9216]{0:T(1024)S(1)} %bitcast.73, f32[9216]{0:T(1024)S(1)} %bitcast.72, f32[9216]{0:T(1024)S(1)} %copy-done.5), kind=kLoop, calls=%fused_computation.16 | loop fusion | flops 7667712 | bytes 10801152 | tf_op jit(solution)/shard_map/convert_element_type | solution.py:26
  51.8 18.7 %all-to-all-done.2 = bf16[8,2,32768]{2,1,0:T(2,128)(2,1)S(1)} async-done(((bf16[8,2,32768]{2,1,0:T(2,128)(2,1)}), bf16[8,2,32768]{2,1,0:T(2,128)(2,1)S(1)}, u32[]{:S(2)}, u32[]{:S(2)}) %all-to-all-start.2) | async-done | bytes 1048608 | tf_op jit(solution)/shard_map/all_to_all | solution.py:48
  70.5 1.0 reshape.173
  71.6 1.2 copy.100
  72.7 1.2 gather_fusion.1
  74.2 1.4 reduce.5
  75.5 1.9 %reshape.174 = bf16[8,2,32768]{2,1,0:T(2,128)(2,1)} reshape(bf16[8,65536]{1,0:T(8,128)(2,1)S(1)} %reduce.5) | data formatting | bytes 2097152
  77.4 3.7 %all-to-all-start.3 = ((bf16[8,2,32768]{2,1,0:T(2,128)(2,1)}), bf16[8,2,32768]{2,1,0:T(2,128)(2,1)S(1)}, u32[]{:S(2)}, u32[]{:S(2)}) async-start(bf16[8,2,32768]{2,1,0:T(2,128)(2,1)} %reshape.174), calls=%async_computation.3 | async-start | bytes 2097152 | tf_op jit(solution)/shard_map/all_to_all | solution.py:54
  81.1 0.7 all-gather.5.cloned.1.call-update
  81.9 2.1 %all_gather.14 = bf16[128,128]{1,0:T(8,128)(2,1)S(1)} all-gather(bf16[64,128]{1,0:T(8,128)(2,1)S(1)} %copy-done.7), channel_id=1, replica_groups=mesh['groups'=2,'dp'=8,'tensor'=2] {'tensor'}, dimensions={0}, use_global_device_ids=true | all-gather | bytes 49152 | tf_op jit(solution)/shard_map/all_gather | solution.py:33
  85.2 0.9 constant_dynamic-slice_fusion.2
  86.3 1.3 constant_dynamic-slice_fusion.1
  87.7 1.3 copy.93
  89.2 2.3 %fusion.1 = bf16[64,128,128]{2,1,0:T(8,128)(2,1)} fusion(f32[64,128]{1,0:T(8,128)S(1)} %copy.77, f32[2,128,128]{2,1,0:T(8,128)S(1)} %fusion.18, f32[64,128]{1,0:T(8,128)S(1)} %copy.73, pred[128,128]{1,0:T(8,128)(4,1)S(1)} %iota_compare_fusion), kind=kLoop, calls=%fused_computation.4 | loop fusion | flops 6291456 | bytes 2310144 | tf_op jit(solution)/shard_map/convert_element_type | solution.py:82
  91.5 15.4 %all-to-all-done.3 = bf16[8,2,32768]{2,1,0:T(2,128)(2,1)S(1)} async-done(((bf16[8,2,32768]{2,1,0:T(2,128)(2,1)}), bf16[8,2,32768]{2,1,0:T(2,128)(2,1)S(1)}, u32[]{:S(2)}, u32[]{:S(2)}) %all-to-all-start.3) | async-done | bytes 1048608 | tf_op jit(solution)/shard_map/all_to_all | solution.py:54
  106.9 1.0 reshape.175
  107.9 4.8 %fusion.10 = bf16[8,65536]{1,0:T(8,128)(2,1)S(1)} fusion(bf16[8,1,65536]{2,1,0:T(2,128)(2,1)S(1)} %reshape.175, pred[]{:T(512)} %bitcast.2), kind=kLoop, calls=%fused_computation.21 | loop fusion | flops 524288 | bytes 2097153 | tf_op jit(solution)/shard_map/jit(_where)/select_n | solution.py:113
  112.7 0.5 select_n.103
  113.3 0.4 fusion.19
  113.7 1.1 copy-done
  115.1 2.9 %fusion.12 = f32[128,64,64]{0,2,1:T(8,128)} fusion(f32[2,32,64,128]{3,2,1,0:T(8,128)S(1)} %fusion.19, bf16[128,64,64]{0,2,1:T(8,128)(2,1)S(1)} %bitcast.64, bf16[64,128,128]{2,1,0:T(8,128)(2,1)S(1)} %copy-done, f32[64]{0:T(128)S(1)} %copy-done.9, f32[128,64]{0,1:T(8,128)S(1)} %copy.81), kind=kOutput, calls=%fused_computation.24 | convolution fusion | flops 136839168 | bytes 7373056 | tf_op jit(solution)/shard_map/htu,uhp->thp/dot_general | solution.py:83
  117.9 1.9 %copy.82 = f32[128,4096]{1,0:T(8,128)S(1)} copy(f32[128,4096]{0,1:T(8,128)} %bitcast.63) | data formatting | bytes 4194304 | tf_op jit(solution)/shard_map/reshape | solution.py:88
  119.9 3.1 %fusion.16 = f32[128,4096]{1,0:T(8,128)} fusion(f32[128,4096]{1,0:T(8,128)S(1)} %copy.82, bf16[128,8192]{1,0:T(8,128)(2,1)} %all-gather.5.cloned.1.call-done, s32[]{:T(128)S(6)} %select_n.104), kind=kLoop, calls=%fused_computation.46 | loop fusion | flops 3670016 | bytes 5242884 | tf_op jit(solution)/shard_map/mul | solution.py:90
  123.0 4.0 %mul.159 = f32[128,2,2048]{2,1,0:T(2,128)} reshape(f32[128,4096]{1,0:T(8,128)} %fusion.16) | data formatting | bytes 4194304 | tf_op jit(solution)/shard_map/mul | solution.py:90
  127.0 2.2 %reduce_sum.9 = f32[128,2]{1,0:T(8,128)S(1)} reduce(f32[128,2,2048]{2,1,0:T(2,128)} %mul.159, f32[]{:T(128)} %constant.62.clone.1), dimensions={2}, to_apply=%region_1.2 | reduce | flops 524032 | bytes 2098180 | tf_op jit(solution)/shard_map/reduce_sum | solution.py:90
  129.3 0.6 mul.160
  129.9 1.7 %copy.96 = f32[16,8,2,2048]{3,1,2,0:T(8,128)S(1)} copy(f32[16,8,2,2048]{3,2,1,0:T(2,128)S(1)} %bitcast.61) | data formatting | bytes 4194304
  131.6 1.8 %select_convert_fusion = bf16[128,4096]{1,0:T(8,128)(2,1)} fusion(f32[128,4096]{1,0:T(8,128)S(1)} %bitcast.60, f32[4096]{0:T(1024)S(1)} %copy-done.6, pred[128]{0:T(512)(128)(4,1)S(1)} %iota_compare_fusion.1, f32[128,4096]{1,0:T(8,128)S(1)} %copy.82, bf16[128,8192]{1,0:T(8,128)(2,1)S(1)} %copy-done.2, s32[]{:T(128)S(6)} %select_n.104), kind=kLoop, calls=%fused_computation.25 | loop fusion | flops 5242880 | bytes 6307972 | tf_op jit(solution)/shard_map/convert_element_type | solution.py:92
  (51 shorter events, 2.9 us)
Async XLA Ops:
  6.5 24.2 %copy-start.4 = (bf16[1,64,64,128]{3,2,1,0:T(8,128)(2,1)S(1)}, bf16[1,64,64,128]{3,2,1,0:T(8,128)(2,1)}, u32[]{:S(2)}) copy-start(bf16[1,64,64,128]{3,2,1,0:T(8,128)(2,1)} %param.23) | copy-start | bytes 3145732
  9.4 13.9 %all-to-all-start = ((bf16[8,2,864]{2,1,0:T(2,128)(2,1)}), bf16[8,2,864]{2,1,0:T(2,128)(2,1)S(1)}, u32[]{:S(2)}, u32[]{:S(2)}) async-start(bf16[8,2,864]{2,1,0:T(2,128)(2,1)} %reshape.176), calls=%async_computation | async-start | bytes 57344 | tf_op jit(solution)/shard_map/all_to_all | solution.py:49
  17.6 30.8 %collective-permute-start = (bf16[3,9216]{1,0:T(4,128)(2,1)S(1)}, bf16[3,9216]{1,0:T(4,128)(2,1)S(1)}, u32[]{:S(2)}, u32[]{:S(2)}) collective-permute-start(bf16[3,9216]{1,0:T(4,128)(2,1)S(1)} %slice.37), channel_id=1, source_target_pairs={{0,1},{2,3},{4,5},{6,7},{8,9},{10,11},{12,13},{14,15},{16,17},{18,... | collective-permute-start | bytes 165896 | tf_op jit(solution)/shard_map/ppermute | solution.py:17
  25.4 14.7 %all-to-all-start.1 = ((bf16[8,2,864]{2,1,0:T(2,128)(2,1)}), bf16[8,2,864]{2,1,0:T(2,128)(2,1)S(1)}, u32[]{:S(2)}, u32[]{:S(2)}) async-start(bf16[8,2,864]{2,1,0:T(2,128)(2,1)} %reshape.178), calls=%async_computation.1 | async-start | bytes 57344 | tf_op jit(solution)/shard_map/all_to_all | solution.py:55
  38.2 10.3 %copy-start.3 = (bf16[64,9216]{1,0:T(8,128)(2,1)S(1)}, bf16[64,9216]{1,0:T(8,128)(2,1)}, u32[]{:S(2)}) copy-start(bf16[64,9216]{1,0:T(8,128)(2,1)} %param.14) | copy-start | bytes 3538948
  40.1 30.5 %all-to-all-start.2 = ((bf16[8,2,32768]{2,1,0:T(2,128)(2,1)}), bf16[8,2,32768]{2,1,0:T(2,128)(2,1)S(1)}, u32[]{:S(2)}, u32[]{:S(2)}) async-start(bf16[8,2,32768]{2,1,0:T(2,128)(2,1)} %reshape.172), calls=%async_computation.2 | async-start | bytes 2097152 | tf_op jit(solution)/shard_map/all_to_all | solution.py:48
  46.0 39.2 %all-gather.3.cloned.1.call-start = ((), (), s32[]{:S(2)}) async-start(), calls=%async_computation.4 | async-start | bytes 3538944 | tf_op jit(solution)/shard_map/all_gather | solution.py:31
  48.5 0.8 copy-start.5
  77.4 4.5 %copy-start.10 = (f32[64]{0:T(128)S(1)}, f32[64]{0:T(128)}, u32[]{:S(2)}) copy-start(f32[64]{0:T(128)} %param.20) | copy-start | bytes 772
  77.4 4.5 %copy-start.7 = (bf16[64,128]{1,0:T(8,128)(2,1)S(1)}, bf16[64,128]{1,0:T(8,128)(2,1)}, u32[]{:S(2)}) copy-start(bf16[64,128]{1,0:T(8,128)(2,1)} %param.16) | copy-start | bytes 49156
  77.4 6.5 %copy-start.8 = (f32[64]{0:T(128)S(1)}, f32[64]{0:T(128)}, u32[]{:S(2)}) copy-start(f32[64]{0:T(128)} %param.19) | copy-start | bytes 772
  77.4 29.5 %all-to-all-start.3 = ((bf16[8,2,32768]{2,1,0:T(2,128)(2,1)}), bf16[8,2,32768]{2,1,0:T(2,128)(2,1)S(1)}, u32[]{:S(2)}, u32[]{:S(2)}) async-start(bf16[8,2,32768]{2,1,0:T(2,128)(2,1)} %reshape.174), calls=%async_computation.3 | async-start | bytes 2097152 | tf_op jit(solution)/shard_map/all_to_all | solution.py:54
  81.1 38.8 %all-gather.5.cloned.1.call-start = ((), (), s32[]{:S(2)}) async-start(), calls=%async_computation.5 | async-start | bytes 3145728 | tf_op jit(solution)/shard_map/all_gather | solution.py:32
  113.2 1.6 %copy-start = (bf16[64,128,128]{2,1,0:T(8,128)(2,1)S(1)}, bf16[64,128,128]{2,1,0:T(8,128)(2,1)}, u32[]{:S(2)}) copy-start(bf16[64,128,128]{2,1,0:T(8,128)(2,1)} %fusion.1) | copy-start | bytes 6291460
  113.2 1.8 %copy-start.1 = (bf16[128,4096]{0,1:T(8,128)(2,1)S(1)}, bf16[128,4096]{0,1:T(8,128)(2,1)}, u32[]{:S(2)}) copy-start(bf16[128,4096]{0,1:T(8,128)(2,1)} %copy.93) | copy-start | bytes 3145732
  113.2 1.8 %copy-start.9 = (f32[64]{0:T(128)S(1)}, f32[64]{0:T(128)}, u32[]{:S(2)}) copy-start(f32[64]{0:T(128)} %param.21) | copy-start | bytes 772
  129.9 1.7 %copy-start.2 = (bf16[128,8192]{1,0:T(8,128)(2,1)S(1)}, bf16[128,8192]{1,0:T(8,128)(2,1)}, u32[]{:S(2)}) copy-start(bf16[128,8192]{1,0:T(8,128)(2,1)} %all-gather.5.cloned.1.call-done) | copy-start | bytes 6291460
  129.9 1.7 %copy-start.6 = (f32[4096]{0:T(1024)S(1)}, f32[4096]{0:T(1024)}, u32[]{:S(2)}) copy-start(f32[4096]{0:T(1024)} %param.22) | copy-start | bytes 49156
Sparse Core Ops, SparseCore 0:
  51.9 12.3 all-gather.2
  83.5 11.9 all-gather.4
where the time goes:
time: 141 us; the launch traced here: 140 us
  waiting for transfers between devices  37.8 us (27%)
  local copies, waits for them, and re-layouts  29.3 us (21%)
  other arithmetic  28.7 us (20%)
  starting transfers between devices  21.8 us (15%)
  between operations  15.1 us (11%)
  blocking collectives  4.09 us (3%)
  matrix products  3.47 us (2%)
    all_to_all x1, waiting for transfers between devices, migrate(): lax.all_to_all(state_flat, 'dp', split_axis=1, concat_axis=0, tiled=True)  18.7 us
    all_to_all x1, waiting for transfers between devices, migrate(): lax.all_to_all(pick_state, 'dp', split_axis=0, concat_axis=1, tiled=True)  15.4 us
    unnamed x37, local copies, waits for them, and re-layouts  14.1 us
    unnamed x2, other arithmetic  7.66 us
    all_to_all x1, starting transfers between devices, migrate(): lax.all_to_all(rims_flat, 'dp', split_axis=1, concat_axis=0, tiled=True)  7.25 us
    all_to_all x1, starting transfers between devices, migrate(): lax.all_to_all(state_flat, 'dp', split_axis=1, concat_axis=0, tiled=True)  5.93 us
    select_n x1, other arithmetic, local(): kept_state = jnp.where(live, kept_state, jnp.zeros_like(kept_state))  4.8 us
    mul x1, local copies, waits for them, and re-layouts, state_space(): grouped * grouped  4.02 us
  transfers between devices with their start and end apart: 7, of which 3 were waited for; matrix products, arithmetic and copies ran while one was open for 31% of the time, Pallas kernels for 0%

commit v1 on v0

v1 whole, which is shorter than its diff:
```python
import functools
import math

import jax
import jax.numpy as jnp
from jax import lax
from jax.experimental import pallas as pl
from jax.experimental.pallas import tpu as pltpu
from jax.sharding import PartitionSpec as P

HEAD_DIM = 64
STATE = 128
NORM_WIDTH = 2048
LANES = 128
EPSILON = 1e-05
LOG2E = math.log2(math.e)
F32 = jnp.float32
BF16 = jnp.bfloat16
MESH = pl.DeviceIdType.MESH
TRANS_B = (((1,), (1,)), ((), ()))


def each(first, last, body):
    if last - first <= 16:
        for index in range(first, last):
            body(index)
    else:
        lax.fori_loop(first, last, lambda index, carry: (body(index), carry)[1], 0)


def silu(value):
    return 0.5 * value * (1.0 + jnp.tanh(0.5 * value))


def kernel(
    n,
    xbc,
    gate,
    dt,
    weight,
    bias,
    dt_bias,
    decay,
    d_skip,
    gain,
    state,
    conv_store,
    source_of,
    prefix_len,
    span_len,
    out,
    x_all,
    gate_all,
    dt_all,
    w_half,
    b_half,
    rim_f32,
    rim_mine,
    rim_held,
    rim_pick,
    rim_got,
    held,
    pick,
    got,
    ext,
    act,
    cum_roll,
    cum_t,
    step_t,
    score,
    fixed,
    factor,
    rim_send1,
    rim_recv1,
    rim_send2,
    rim_recv2,
    send1,
    recv1,
    send2,
    recv2,
    pair_send,
    pair_recv,
    local_sem,
    own_sem,
):
    me = lax.axis_index("dp")
    core = lax.axis_index("tensor")
    mate = 1 - core
    rows = xbc.shape[0]
    count = x_all.shape[0]
    half = x_all.shape[1]
    inner = gate_all.shape[1]
    chunks, _, piece, _ = pick.shape
    groups = (half - inner) // (2 * STATE)
    rim_count = conv_store.shape[1]
    tiles = half // LANES

    here = pl.ds(pl.multiple_of(core * rows, rows), rows)
    own_x = pl.ds(pl.multiple_of(core * half, LANES), half)
    own_z = pl.ds(pl.multiple_of(core * inner, LANES), inner)
    local = [
        pltpu.make_async_copy(xbc.at[:, own_x], x_all.at[here, :], local_sem.at[0]),
        pltpu.make_async_copy(gate.at[:, own_z], gate_all.at[here, :], local_sem.at[1]),
        pltpu.make_async_copy(dt, dt_all.at[here, :], local_sem.at[2]),
        pltpu.make_async_copy(weight.at[:, own_x], w_half, local_sem.at[3]),
        pltpu.make_async_copy(bias.at[:, own_x], b_half, local_sem.at[4]),
    ]
    for copy in local:
        copy.start()

    def own_state(c):
        begin = pl.multiple_of((c * n + me) * piece, piece)
        return pltpu.make_async_copy(
            state.at[pl.ds(begin, piece), :], held[c].at[me], own_sem.at[c]
        )

    for c in range(chunks):
        own_state(c).start()

    barrier = pltpu.get_barrier_semaphore()

    def greet(step):
        pl.semaphore_signal(
            barrier, inc=1, device_id={"dp": lax.rem(me + step, n)}, device_id_type=MESH
        )

    each(1, n, greet)
    pl.semaphore_signal(barrier, inc=1, device_id={"tensor": mate}, device_id_type=MESH)

    rim_f32[...] = jnp.zeros_like(rim_f32)
    for i in range(rim_count):
        line = conv_store[0, pl.ds(i, 1), :].astype(F32)
        for j in range(tiles):
            rim_f32[pl.ds(i * tiles + j, 1), :] = line[:, j * LANES : (j + 1) * LANES]
    rim_mine[...] = rim_f32[...].astype(BF16).reshape(rim_mine.shape)
    rim_held[me] = rim_mine[me]

    pl.semaphore_wait(barrier, n)

    def rims1(peer, slot):
        return pltpu.make_async_remote_copy(
            src_ref=rim_mine.at[peer],
            dst_ref=rim_held.at[slot],
            send_sem=rim_send1.at[peer],
            recv_sem=rim_recv1.at[slot],
            device_id={"dp": peer},
            device_id_type=MESH,
        )

    def rims2(peer, slot):
        return pltpu.make_async_remote_copy(
            src_ref=rim_pick.at[peer],
            dst_ref=rim_got.at[slot],
            send_sem=rim_send2.at[peer],
            recv_sem=rim_recv2.at[slot],
            device_id={"dp": peer},
            device_id_type=MESH,
        )

    def states1(c, peer, slot):
        begin = pl.multiple_of((c * n + peer) * piece, piece)
        return pltpu.make_async_remote_copy(
            src_ref=state.at[pl.ds(begin, piece), :],
            dst_ref=held[c].at[slot],
            send_sem=send1.at[c, peer],
            recv_sem=recv1.at[c, slot],
            device_id={"dp": peer},
            device_id_type=MESH,
        )

    def states2(c, peer, slot):
        return pltpu.make_async_remote_copy(
            src_ref=pick.at[c, peer],
            dst_ref=got.at[c, slot],
            send_sem=send2.at[c, peer],
            recv_sem=recv2.at[c, slot],
            device_id={"dp": peer},
            device_id_type=MESH,
        )

    def peer_at(step):
        return lax.rem(me + step, n)

    each(1, n, lambda s: rims1(peer_at(s), me).start())

    other_x = pl.ds(pl.multiple_of(mate * half, LANES), half)
    other_z = pl.ds(pl.multiple_of(mate * inner, LANES), inner)

    def pair(index, source, target):
        return pltpu.make_async_remote_copy(
            src_ref=source,
            dst_ref=target,
            send_sem=pair_send.at[index],
            recv_sem=pair_recv.at[index],
            device_id={"tensor": mate},
            device_id_type=MESH,
        )

    exchange = [
        pair(0, dt, dt_all.at[here, :]),
        pair(1, xbc.at[:, other_x], x_all.at[here, :]),
        pair(2, gate.at[:, other_z], gate_all.at[here, :]),
    ]
    for copy in exchange:
        copy.start()
    for c in range(chunks):
        each(1, n, functools.partial(lambda c, s: states1(c, peer_at(s), me).start(), c))

    each(1, n, lambda s: rims1(peer_at(s), peer_at(s)).wait_recv())

    def choose_rims(d):
        rim_pick[d] = rim_held[source_of[d]]

    each(0, n, choose_rims)
    rim_got[me] = rim_pick[me]
    each(1, n, lambda s: rims2(peer_at(s), me).start())

    for copy in local:
        copy.wait()
    for copy in exchange:
        copy.wait()
    both = dt_all[...].astype(F32)
    mine = jnp.where(core == 0, both, pltpu.roll(both, LANES // 2, 1))
    twice = lambda ref: jnp.concatenate([ref[...], ref[...]], axis=1)
    raised = mine + twice(dt_bias)
    step_size = jnp.maximum(raised, 0.0) + jnp.log1p(jnp.exp(-jnp.abs(raised)))
    t_index = lax.broadcasted_iota(jnp.int32, (count, count), 0)
    u_index = lax.broadcasted_iota(jnp.int32, (count, count), 1)
    lower = (t_index >= u_index).astype(F32)
    cum = jnp.dot(
        lower,
        -twice(decay) * step_size,
        precision=lax.Precision.HIGHEST,
        preferred_element_type=F32,
    )
    cum = cum * LOG2E
    cum_roll[...] = cum
    cum_t[...] = cum.T
    step_t[...] = step_size.T
    live = jnp.where(prefix_len[0] > 0, 1.0, 0.0)

    each(1, n, lambda s: rims2(peer_at(s), peer_at(s)).wait_recv())
    rim_f32[...] = rim_got[...].reshape(rim_f32.shape).astype(F32) * live

    width = ext.shape[1]
    per = width // LANES

    def convolve(j, carry):
        columns = pl.ds(pl.multiple_of(j * width, width), width)
        for i in range(rim_count):
            for m in range(per):
                ext[pl.ds(8 - rim_count + i, 1), m * LANES : (m + 1) * LANES] = rim_f32[
                    pl.ds(i * tiles + j * per + m, 1), :
                ]
        ext[pl.ds(8, count), :] = x_all[:, columns].astype(F32)
        total = b_half[:, columns]
        for k in range(rim_count + 1):
            total = total + w_half[pl.ds(k, 1), columns] * ext[pl.ds(8 - rim_count + k, count), :]
        act[:, columns] = silu(total).astype(BF16)
        return carry

    lax.fori_loop(0, half // width, convolve, 0)

    for g in range(groups):
        b_proj = act[:, inner + g * STATE : inner + (g + 1) * STATE]
        c_proj = act[:, inner + (groups + g) * STATE : inner + (groups + g + 1) * STATE]
        score[g] = lax.dot_general(c_proj, b_proj, TRANS_B, preferred_element_type=F32)

    pairs = inner // LANES
    first_head = lax.broadcasted_iota(jnp.int32, (count, LANES), 1) < HEAD_DIM
    causal = t_index >= u_index

    def inside(q, carry):
        columns = pl.ds(pl.multiple_of(q * LANES, LANES), LANES)
        cum_now = cum_roll[...]
        scores = score[q // (pairs // groups)]
        weights = []
        edges = []
        for m in range(2):
            edge = jnp.broadcast_to(cum_now[:, m : m + 1], (count, count))
            spread = edge - cum_t[pl.ds(2 * q + m, 1), :]
            fall = jnp.exp2(jnp.where(causal, spread, -1e30))
            weights.append((fall * scores * step_t[pl.ds(2 * q + m, 1), :]).astype(BF16))
            edges.append(edge)
        cum_roll[...] = pltpu.roll(cum_now, LANES - 2, 1)
        x_now = act[:, columns]
        none = jnp.zeros_like(x_now)
        stacked = jnp.concatenate(
            [jnp.where(first_head, x_now, none), jnp.where(first_head, none, x_now)], axis=0
        )
        intra = jnp.dot(
            jnp.concatenate(weights, axis=1), stacked, preferred_element_type=F32
        )
        skip = jnp.where(first_head, d_skip[2 * q], d_skip[2 * q + 1])
        open_gate = silu(gate_all[:, columns].astype(F32))
        fixed[:, columns] = (intra + skip * x_now.astype(F32)) * open_gate
        carry_in = jnp.exp2(jnp.where(first_head, edges[0], edges[1])) * live
        factor[:, columns] = carry_in * open_gate
        return carry

    def choose(c):
        own_state(c).wait()
        each(1, n, lambda s: states1(c, peer_at(s), peer_at(s)).wait_recv())

        def choose_one(d):
            pick[c, d] = held[c][source_of[d]]

        each(0, n, choose_one)
        got[c, me] = pick[c, me]
        each(1, n, lambda s: states2(c, peer_at(s), me).start())

    per_chunk = pairs // chunks
    for c in range(chunks):
        lax.fori_loop(c * per_chunk, (c + 1) * per_chunk, inside, 0)
        choose(c)

    alive = lax.broadcasted_iota(jnp.int32, (count, 1), 0) < span_len[0]
    block = inner // chunks
    for c in range(chunks):
        c_proj = act[:, inner + (groups + c) * STATE : inner + (groups + c + 1) * STATE]
        each(1, n, lambda s: states2(c, peer_at(s), peer_at(s)).wait_recv())
        kept = got[c].reshape(block, STATE)
        wide = 256
        total = jnp.zeros((count, LANES), F32)
        for b in range(block // wide):
            columns = slice(c * block + b * wide, c * block + (b + 1) * wide)
            carried = lax.dot_general(
                c_proj,
                kept[b * wide : (b + 1) * wide],
                TRANS_B,
                preferred_element_type=F32,
            )
            gated = fixed[:, columns] + carried * factor[:, columns]
            fixed[:, columns] = gated
            square = gated * gated
            for m in range(wide // LANES):
                total = total + square[:, m * LANES : (m + 1) * LANES]
        mean = jnp.sum(total, axis=1, keepdims=True) * (1.0 / block)
        scale = jnp.where(alive, lax.rsqrt(mean + EPSILON), 0.0)
        for b in range(block // wide):
            columns = slice(c * block + b * wide, c * block + (b + 1) * wide)
            out[:, columns] = (fixed[:, columns] * scale * gain[:, columns]).astype(BF16)

    each(1, n, lambda s: rims1(peer_at(s), me).wait_send())
    each(1, n, lambda s: rims2(peer_at(s), me).wait_send())
    for c in range(chunks):
        each(1, n, functools.partial(lambda c, s: states1(c, peer_at(s), me).wait_send(), c))
        each(1, n, functools.partial(lambda c, s: states2(c, peer_at(s), me).wait_send(), c))


def local(
    n,
    xbc,
    gate_z,
    dt_raw,
    conv_weight,
    conv_bias,
    dt_bias,
    decay_rate,
    d_skip,
    norm_gain,
    ssm_store,
    conv_store,
    source_of,
    prefix_len,
    span_len,
):
    rows = xbc.shape[0]
    count = 2 * rows
    half = xbc.shape[1] // 2
    inner = gate_z.shape[1] // 2
    chunks = inner // NORM_WIDTH
    piece = inner // (chunks * n)
    tiles = half // LANES
    rim_piece = 16 * pl.cdiv(conv_store.shape[1] * tiles, 16 * n)
    vmem = pl.BlockSpec(memory_space=pltpu.VMEM)
    smem = pl.BlockSpec(memory_space=pltpu.SMEM)
    hbm = pl.BlockSpec(memory_space=pl.ANY)
    width = 512
    dma = pltpu.SemaphoreType.DMA
    return pl.pallas_call(
        functools.partial(kernel, n),
        out_shape=jax.ShapeDtypeStruct((count, inner), BF16),
        in_specs=[
            hbm, hbm, hbm, hbm, hbm, vmem, vmem, smem, vmem, hbm, vmem, smem, smem, smem,
        ],
        out_specs=vmem,
        scratch_shapes=[
            pltpu.VMEM((count, half), BF16),
            pltpu.VMEM((count, inner), BF16),
            pltpu.VMEM((count, dt_raw.shape[1]), BF16),
            pltpu.VMEM((conv_weight.shape[0], half), F32),
            pltpu.VMEM((1, half), F32),
            pltpu.VMEM((n * rim_piece, LANES), F32),
            pltpu.VMEM((n, rim_piece, LANES), BF16),
            pltpu.VMEM((n, rim_piece, LANES), BF16),
            pltpu.VMEM((n, rim_piece, LANES), BF16),
            pltpu.VMEM((n, rim_piece, LANES), BF16),
            [pltpu.VMEM((n, piece, STATE), BF16) for _ in range(chunks)],
            pltpu.VMEM((chunks, n, piece, STATE), BF16),
            pltpu.VMEM((chunks, n, piece, STATE), BF16),
            pltpu.VMEM((8 + count, width), F32),
            pltpu.VMEM((count, half), BF16),
            pltpu.VMEM((count, LANES), F32),
            pltpu.VMEM((LANES, count), F32),
            pltpu.VMEM((LANES, count), F32),
            pltpu.VMEM(((half - inner) // (2 * STATE), count, count), F32),
            pltpu.VMEM((count, inner), F32),
            pltpu.VMEM((count, inner), F32),
            dma((n,)),
            dma((n,)),
            dma((n,)),
            dma((n,)),
            dma((chunks, n)),
            dma((chunks, n)),
            dma((chunks, n)),
            dma((chunks, n)),
            dma((3,)),
            dma((3,)),
            dma((5,)),
            dma((chunks,)),
        ],
        compiler_params=pltpu.CompilerParams(
            collective_id=0, has_side_effects=True, vmem_limit_bytes=48 * 1024 * 1024
        ),
    )(
        xbc,
        gate_z,
        dt_raw,
        conv_weight,
        conv_bias.reshape(1, -1),
        dt_bias.reshape(1, -1),
        decay_rate.reshape(1, -1),
        d_skip,
        norm_gain.reshape(1, -1),
        ssm_store.reshape(-1, STATE),
        conv_store,
        source_of,
        prefix_len,
        span_len,
    )


def solution(mesh):
    in_specs = (
        P(("groups", "dp", "tensor"), None),
        P(("groups", "dp", "tensor"), None),
        P(("groups", "dp", "tensor"), None),
        P(),
        P(),
        P("tensor"),
        P("tensor"),
        P("tensor"),
        P("tensor"),
        P(("groups", "dp"), "tensor", None, None),
        P(("groups", "dp"), None, "tensor"),
        P("groups"),
        P(("groups", "dp")),
        P(("groups", "dp")),
    )
    out_specs = P(("groups", "dp"), "tensor")
    return jax.shard_map(
        functools.partial(local, mesh.shape["dp"]),
        mesh=mesh,
        in_specs=in_specs,
        out_specs=out_specs,
        check_vma=False,
    )
```

time: 141 us -> 74.7 us (0.53)
  Pallas kernels: 0 us -> 61.6 us
  waiting for transfers between devices: 37.8 us -> 0 us
  other arithmetic: 28.7 us -> 0 us
  starting transfers between devices: 21.8 us -> 0 us
  local copies, waits for them, and re-layouts: 29.3 us -> 11.2 us
  between operations: 15.1 us -> 1.32 us
  blocking collectives: 4.09 us -> 0 us
  matrix products: 3.47 us -> 0 us
    pallas_call x0 -> x1, Pallas kernels: none -> 61.6 us  [local(): pl.pallas_call(functools.partial(kernel, n), out_shape=jax.ShapeDtypeStru...]
    all_to_all x4 -> x0, waiting for transfers between devices: 37 us -> none  [the longest x1 18.7 us: migrate(): lax.all_to_all(state_flat, 'dp', split_axis=1, concat_axis=0, tiled=True)]
    all_to_all x4 -> x0, starting transfers between devices: 20.2 us -> none  [the longest x1 7.25 us: migrate(): lax.all_to_all(rims_flat, 'dp', split_axis=1, concat_axis=0, tiled=True)]
    select_n x8 -> x0, other arithmetic: 7.8 us -> none  [the longest x1 4.8 us: local(): kept_state = jnp.where(live, kept_state, jnp.zeros_like(kept_state))]
    unnamed x2 -> x0, other arithmetic: 7.66 us -> none
    convert_element_type x4 -> x0, other arithmetic: 6.96 us -> none  [the longest x1 2.55 us: convolve(): return jax.nn.silu(total).astype(jnp.bfloat16)]
    mul x2 -> x0, local copies, waits for them, and re-layouts: 4.62 us -> none  [the longest x1 4.02 us: state_space(): grouped * grouped]
    slice x4 -> x0, local copies, waits for them, and re-layouts: 4.48 us -> none  [the longest x1 1.34 us: convolve(): total = total + weight[offset][None, :] * extended[offset:offset + count]]
  transfers between devices with their start and end apart: 7 -> 0, of which waited for: 3 -> 0; matrix products, arithmetic and copies ran while one was open for 31% -> 0% of each run, Pallas kernels for 0% -> 0%
where the time goes in v1:
time: 74.7 us; the launch traced here: 74.1 us
  Pallas kernels  61.6 us (82%)
  local copies, waits for them, and re-layouts  11.2 us (15%)
  between operations  1.32 us (2%)
    pallas_call x1, Pallas kernels, local(): pl.pallas_call(functools.partial(kernel, n), out_shape=jax.ShapeDtypeStru...  61.6 us
    unnamed x25, local copies, waits for them, and re-layouts  11.2 us

profile of v1, /device:TPU:0, one launch (start us, length us, event | category | flops | bytes accessed | tf_op | source)
XLA Modules:
  0.0 74.1 jit_solution(11880550567597024315)
XLA Ops:
  1.3 0.0 copy-start
  1.3 1.3 %copy-done = bf16[64,9216]{1,0:T(8,128)(2,1)S(1)} copy-done((bf16[64,9216]{1,0:T(8,128)(2,1)S(1)}, bf16[64,9216]{1,0:T(8,128)(2,1)}, u32[]{:S(2)}) %copy-start) | copy-done | bytes 1179672
  2.6 0.0 copy-start.1
  2.6 1.2 %copy-done.1 = bf16[64,8192]{1,0:T(8,128)(2,1)S(1)} copy-done((bf16[64,8192]{1,0:T(8,128)(2,1)S(1)}, bf16[64,8192]{1,0:T(8,128)(2,1)}, u32[]{:S(2)}) %copy-start.1) | copy-done | bytes 1048600
  3.8 0.0 copy-start.2
  3.8 1.2 %copy-done.2 = bf16[1,64,64,128]{3,2,1,0:T(8,128)(2,1)S(1)} copy-done((bf16[1,64,64,128]{3,2,1,0:T(8,128)(2,1)S(1)}, bf16[1,64,64,128]{3,2,1,0:T(8,128)(2,1)}, u32[]{:S(2)}) %copy-start.2) | copy-done | bytes 1048600
  5.0 0.0 copy-start.3
  5.0 0.9 %copy-done.3 = f32[4,9216]{1,0:T(4,128)S(1)} copy-done((f32[4,9216]{1,0:T(4,128)S(1)}, f32[4,9216]{1,0:T(4,128)}, u32[]{:S(2)}) %copy-start.3) | copy-done | bytes 147480
  5.9 0.0 copy-start.4
  5.9 0.8 %copy-done.4 = f32[9216]{0:T(1024)S(1)} copy-done((f32[9216]{0:T(1024)S(1)}, f32[9216]{0:T(1024)}, u32[]{:S(2)}) %copy-start.4) | copy-done | bytes 36888
  6.7 0.0 copy-start.5
  6.7 0.8 %copy-done.5 = bf16[1,3,4608]{2,1,0:T(4,128)(2,1)S(1)} copy-done((bf16[1,3,4608]{2,1,0:T(4,128)(2,1)S(1)}, bf16[1,3,4608]{2,1,0:T(4,128)(2,1)}, u32[]{:S(2)}) %copy-start.5) | copy-done | bytes 27672
  7.5 0.0 copy-start.6
  7.5 0.7 copy-done.6
  8.2 0.0 copy-start.7
  8.2 0.7 copy-done.7
  8.9 0.0 copy-start.8
  8.9 0.7 copy-done.8
  9.6 0.0 copy-start.9
  9.6 0.7 copy-done.9
  10.2 0.0 copy-start.10
  10.2 0.7 copy-done.10
  10.9 0.0 copy-start.11
  10.9 0.7 copy-done.11
  11.5 61.6 %shard_map.136 = bf16[128,4096]{1,0:T(8,128)(2,1)S(1)} custom-call(bf16[64,9216]{1,0:T(8,128)(2,1)S(1)} %copy-done, bf16[64,8192]{1,0:T(8,128)(2,1)S(1)} %copy-done.1, bf16[64,128]{1,0:T(8,128)(2,1)S(1)} %copy-done.6, f32[4,9216]{1,0:T(4,128)S(1)} %copy-done.3, f32[1,9216]{1,0:T(1,128)S(1)} %bitcast.6, f32[1,64]{1,0:T(1,128)S(1)} %bitcast.8, ...), custom_call_target="tpu_custom_call" | custom-call | tf_op jit(solution)/shard_map/pallas_call | solution.py:381
  73.2 1.0 %copy.18 = bf16[128,4096]{1,0:T(8,128)(2,1)} copy(bf16[128,4096]{1,0:T(8,128)(2,1)S(1)} %shard_map.136) | data formatting | bytes 2097152
Async XLA Ops:
  1.3 1.3 %copy-start = (bf16[64,9216]{1,0:T(8,128)(2,1)S(1)}, bf16[64,9216]{1,0:T(8,128)(2,1)}, u32[]{:S(2)}) copy-start(bf16[64,9216]{1,0:T(8,128)(2,1)} %xbc.1) | copy-start | bytes 3538948
  2.6 1.2 %copy-start.1 = (bf16[64,8192]{1,0:T(8,128)(2,1)S(1)}, bf16[64,8192]{1,0:T(8,128)(2,1)}, u32[]{:S(2)}) copy-start(bf16[64,8192]{1,0:T(8,128)(2,1)} %gate.1) | copy-start | bytes 3145732
  3.8 1.2 %copy-start.2 = (bf16[1,64,64,128]{3,2,1,0:T(8,128)(2,1)S(1)}, bf16[1,64,64,128]{3,2,1,0:T(8,128)(2,1)}, u32[]{:S(2)}) copy-start(bf16[1,64,64,128]{3,2,1,0:T(8,128)(2,1)} %param.23) | copy-start | bytes 3145732
  5.0 0.9 %copy-start.3 = (f32[4,9216]{1,0:T(4,128)S(1)}, f32[4,9216]{1,0:T(4,128)}, u32[]{:S(2)}) copy-start(f32[4,9216]{1,0:T(4,128)} %weight.1) | copy-start | bytes 442372
  5.9 0.8 %copy-start.4 = (f32[9216]{0:T(1024)S(1)}, f32[9216]{0:T(1024)}, u32[]{:S(2)}) copy-start(f32[9216]{0:T(1024)} %param.18) | copy-start | bytes 110596
  6.7 0.8 %copy-start.5 = (bf16[1,3,4608]{2,1,0:T(4,128)(2,1)S(1)}, bf16[1,3,4608]{2,1,0:T(4,128)(2,1)}, u32[]{:S(2)}) copy-start(bf16[1,3,4608]{2,1,0:T(4,128)(2,1)} %conv_store.1) | copy-start | bytes 82948
  7.5 0.7 copy-start.6
  8.2 0.7 copy-start.7
  8.9 0.7 copy-start.8
  9.6 0.7 copy-start.9
  10.2 0.7 copy-start.10
  10.9 0.7 copy-start.11

commit v2 on v1

--- a/solution.py
+++ b/solution.py
@@ -82,6 +82,9 @@
     pair_recv,
     local_sem,
     own_sem,
+    dt_bias_v,
+    decay_v,
+    gain_v,
 ):
     me = lax.axis_index("dp")
     core = lax.axis_index("tensor")
@@ -104,6 +107,9 @@
         pltpu.make_async_copy(dt, dt_all.at[here, :], local_sem.at[2]),
         pltpu.make_async_copy(weight.at[:, own_x], w_half, local_sem.at[3]),
         pltpu.make_async_copy(bias.at[:, own_x], b_half, local_sem.at[4]),
+        pltpu.make_async_copy(dt_bias, dt_bias_v, local_sem.at[5]),
+        pltpu.make_async_copy(decay, decay_v, local_sem.at[6]),
+        pltpu.make_async_copy(gain, gain_v, local_sem.at[7]),
     ]
     for copy in local:
         copy.start()
@@ -203,8 +209,11 @@
     ]
     for copy in exchange:
         copy.start()
-    for c in range(chunks):
-        each(1, n, functools.partial(lambda c, s: states1(c, peer_at(s), me).start(), c))
+
+    def spread_out(c):
+        each(1, n, lambda s: states1(c, peer_at(s), me).start())
+
+    spread_out(0)
 
     each(1, n, lambda s: rims1(peer_at(s), peer_at(s)).wait_recv())
 
@@ -214,6 +223,8 @@
     each(0, n, choose_rims)
     rim_got[me] = rim_pick[me]
     each(1, n, lambda s: rims2(peer_at(s), me).start())
+    for c in range(1, chunks):
+        spread_out(c)
 
     for copy in local:
         copy.wait()
@@ -222,14 +233,14 @@
     both = dt_all[...].astype(F32)
     mine = jnp.where(core == 0, both, pltpu.roll(both, LANES // 2, 1))
     twice = lambda ref: jnp.concatenate([ref[...], ref[...]], axis=1)
-    raised = mine + twice(dt_bias)
+    raised = mine + twice(dt_bias_v)
     step_size = jnp.maximum(raised, 0.0) + jnp.log1p(jnp.exp(-jnp.abs(raised)))
     t_index = lax.broadcasted_iota(jnp.int32, (count, count), 0)
     u_index = lax.broadcasted_iota(jnp.int32, (count, count), 1)
     lower = (t_index >= u_index).astype(F32)
     cum = jnp.dot(
         lower,
-        -twice(decay) * step_size,
+        -twice(decay_v) * step_size,
         precision=lax.Precision.HIGHEST,
         preferred_element_type=F32,
     )
@@ -238,6 +249,19 @@
     cum_t[...] = cum.T
     step_t[...] = step_size.T
     live = jnp.where(prefix_len[0] > 0, 1.0, 0.0)
+
+    def choose(c):
+        own_state(c).wait()
+        each(1, n, lambda s: states1(c, peer_at(s), peer_at(s)).wait_recv())
+
+        def choose_one(d):
+            pick[c, d] = held[c][source_of[d]]
+
+        each(0, n, choose_one)
+        got[c, me] = pick[c, me]
+        each(1, n, lambda s: states2(c, peer_at(s), me).start())
+
+    choose(0)
 
     each(1, n, lambda s: rims2(peer_at(s), peer_at(s)).wait_recv())
     rim_f32[...] = rim_got[...].reshape(rim_f32.shape).astype(F32) * live
@@ -298,21 +322,11 @@
         factor[:, columns] = carry_in * open_gate
         return carry
 
-    def choose(c):
-        own_state(c).wait()
-        each(1, n, lambda s: states1(c, peer_at(s), peer_at(s)).wait_recv())
-
-        def choose_one(d):
-            pick[c, d] = held[c][source_of[d]]
-
-        each(0, n, choose_one)
-        got[c, me] = pick[c, me]
-        each(1, n, lambda s: states2(c, peer_at(s), me).start())
-
     per_chunk = pairs // chunks
     for c in range(chunks):
         lax.fori_loop(c * per_chunk, (c + 1) * per_chunk, inside, 0)
-        choose(c)
+        if c + 1 < chunks:
+            choose(c + 1)
 
     alive = lax.broadcasted_iota(jnp.int32, (count, 1), 0) < span_len[0]
     block = inner // chunks
@@ -339,7 +353,7 @@
         scale = jnp.where(alive, lax.rsqrt(mean + EPSILON), 0.0)
         for b in range(block // wide):
             columns = slice(c * block + b * wide, c * block + (b + 1) * wide)
-            out[:, columns] = (fixed[:, columns] * scale * gain[:, columns]).astype(BF16)
+            out[:, columns] = (fixed[:, columns] * scale * gain_v[:, columns]).astype(BF16)
 
     each(1, n, lambda s: rims1(peer_at(s), me).wait_send())
     each(1, n, lambda s: rims2(peer_at(s), me).wait_send())
@@ -382,7 +396,7 @@
         functools.partial(kernel, n),
         out_shape=jax.ShapeDtypeStruct((count, inner), BF16),
         in_specs=[
-            hbm, hbm, hbm, hbm, hbm, vmem, vmem, smem, vmem, hbm, vmem, smem, smem, smem,
+            hbm, hbm, hbm, hbm, hbm, hbm, hbm, smem, hbm, hbm, vmem, smem, smem, smem,
         ],
         out_specs=vmem,
         scratch_shapes=[
@@ -417,11 +431,14 @@
             dma((chunks, n)),
             dma((3,)),
             dma((3,)),
-            dma((5,)),
+            dma((8,)),
             dma((chunks,)),
+            pltpu.VMEM((1, inner // HEAD_DIM), F32),
+            pltpu.VMEM((1, inner // HEAD_DIM), F32),
+            pltpu.VMEM((1, inner), F32),
         ],
         compiler_params=pltpu.CompilerParams(
-            collective_id=0, has_side_effects=True, vmem_limit_bytes=48 * 1024 * 1024
+            collective_id=0, has_side_effects=True, vmem_limit_bytes=60 * 1024 * 1024
         ),
     )(
         xbc,

time: 74.7 us -> 58.3 us (0.78)
  the two profiles are of different devices: /device:TPU:0 before, /device:TPU:15 now
where the time goes in v2:
time: 58.3 us; the launch traced here: 58.1 us
  Pallas kernels  54.5 us (93%)
  local copies, waits for them, and re-layouts  2.29 us (4%)
  between operations  1.3 us (2%)
    pallas_call x1, Pallas kernels, local(): pl.pallas_call(functools.partial(kernel, n), out_shape=jax.ShapeDtypeStru...  54.5 us
    unnamed x1, local copies, waits for them, and re-layouts  2.29 us

profile of v2, /device:TPU:15, one launch (start us, length us, event | category | flops | bytes accessed | tf_op | source)
XLA Modules:
  0.0 58.1 jit_solution(1322622027773509435)
XLA Ops:
  1.3 54.5 %shard_map.136 = bf16[128,4096]{1,0:T(8,128)(2,1)} custom-call(bf16[64,9216]{1,0:T(8,128)(2,1)} %xbc.1, bf16[64,8192]{1,0:T(8,128)(2,1)} %gate.1, bf16[64,128]{1,0:T(8,128)(2,1)} %dt.1, f32[4,9216]{1,0:T(4,128)} %weight.1, f32[1,9216]{1,0:T(1,128)} %bitcast.6, f32[1,64]{1,0:T(1,128)} %bitcast.8, f32[1,64]{1,0:T(1,128)} %bitcast.9, f32[64]{0:T(128)} %d_skip.1, ...), custom_call_target="tpu_custom_call" | custom-call | tf_op jit(solution)/shard_map/pallas_call | solution.py:395
  55.8 2.3 %copy.18 = bf16[128,4096]{1,0:T(8,128)(2,1)} copy(bf16[128,4096]{1,0:T(8,128)(2,1)} %shard_map.136) | data formatting | bytes 2097152

commit v3 on v2

--- a/solution.py
+++ b/solution.py
@@ -41,13 +41,13 @@
     bias,
     dt_bias,
     decay,
-    d_skip,
+    d_skip_h,
     gain,
     state,
-    conv_store,
-    source_of,
-    prefix_len,
-    span_len,
+    conv_h,
+    source_h,
+    prefix_h,
+    span_h,
     out,
     x_all,
     gate_all,
@@ -85,6 +85,12 @@
     dt_bias_v,
     decay_v,
     gain_v,
+    d_skip,
+    source_of,
+    prefix_len,
+    span_len,
+    conv_store,
+    small_sem,
 ):
     me = lax.axis_index("dp")
     core = lax.axis_index("tensor")
@@ -97,6 +103,26 @@
     groups = (half - inner) // (2 * STATE)
     rim_count = conv_store.shape[1]
     tiles = half // LANES
+
+    barrier = pltpu.get_barrier_semaphore()
+
+    def greet(step):
+        pl.semaphore_signal(
+            barrier, inc=1, device_id={"dp": lax.rem(me + step, n)}, device_id_type=MESH
+        )
+
+    each(1, n, greet)
+    pl.semaphore_signal(barrier, inc=1, device_id={"tensor": mate}, device_id_type=MESH)
+
+    small = [
+        pltpu.make_async_copy(conv_h, conv_store, small_sem.at[0]),
+        pltpu.make_async_copy(source_h, source_of, small_sem.at[1]),
+        pltpu.make_async_copy(d_skip_h, d_skip, small_sem.at[2]),
+        pltpu.make_async_copy(prefix_h, prefix_len, small_sem.at[3]),
+        pltpu.make_async_copy(span_h, span_len, small_sem.at[4]),
+    ]
+    for copy in small:
+        copy.start()
 
     here = pl.ds(pl.multiple_of(core * rows, rows), rows)
     own_x = pl.ds(pl.multiple_of(core * half, LANES), half)
@@ -123,17 +149,9 @@
     for c in range(chunks):
         own_state(c).start()
 
-    barrier = pltpu.get_barrier_semaphore()
-
-    def greet(step):
-        pl.semaphore_signal(
-            barrier, inc=1, device_id={"dp": lax.rem(me + step, n)}, device_id_type=MESH
-        )
-
-    each(1, n, greet)
-    pl.semaphore_signal(barrier, inc=1, device_id={"tensor": mate}, device_id_type=MESH)
-
     rim_f32[...] = jnp.zeros_like(rim_f32)
+    for copy in small:
+        copy.wait()
     for i in range(rim_count):
         line = conv_store[0, pl.ds(i, 1), :].astype(F32)
         for j in range(tiles):
@@ -184,8 +202,17 @@
             device_id_type=MESH,
         )
 
+    bits = n.bit_length() - 1
+
     def peer_at(step):
-        return lax.rem(me + step, n)
+        if n & (n - 1):
+            return lax.rem(me + step, n)
+        flip = (step + 1) // 2 + (step % 2) * (n // 2 - 1)
+        peer = 0
+        for b in range(bits):
+            weight_b = 1 << b
+            peer = peer + weight_b * ((me // weight_b + flip // weight_b) % 2)
+        return peer
 
     each(1, n, lambda s: rims1(peer_at(s), me).start())
 
@@ -389,14 +416,14 @@
     rim_piece = 16 * pl.cdiv(conv_store.shape[1] * tiles, 16 * n)
     vmem = pl.BlockSpec(memory_space=pltpu.VMEM)
     smem = pl.BlockSpec(memory_space=pltpu.SMEM)
-    hbm = pl.BlockSpec(memory_space=pl.ANY)
+    hbm = pl.BlockSpec(memory_space=pltpu.HBM)
     width = 512
     dma = pltpu.SemaphoreType.DMA
     return pl.pallas_call(
         functools.partial(kernel, n),
         out_shape=jax.ShapeDtypeStruct((count, inner), BF16),
         in_specs=[
-            hbm, hbm, hbm, hbm, hbm, hbm, hbm, smem, hbm, hbm, vmem, smem, smem, smem,
+            hbm, hbm, hbm, hbm, hbm, hbm, hbm, hbm, hbm, hbm, hbm, hbm, hbm, hbm,
         ],
         out_specs=vmem,
         scratch_shapes=[
@@ -436,6 +463,12 @@
             pltpu.VMEM((1, inner // HEAD_DIM), F32),
             pltpu.VMEM((1, inner // HEAD_DIM), F32),
             pltpu.VMEM((1, inner), F32),
+            pltpu.SMEM(d_skip.shape, F32),
+            pltpu.SMEM(source_of.shape, jnp.int32),
+            pltpu.SMEM(prefix_len.shape, jnp.int32),
+            pltpu.SMEM(span_len.shape, jnp.int32),
+            pltpu.VMEM(conv_store.shape, BF16),
+            dma((5,)),
         ],
         compiler_params=pltpu.CompilerParams(
             collective_id=0, has_side_effects=True, vmem_limit_bytes=60 * 1024 * 1024

time: 58.3 us -> 58 us (level)
  the two profiles are of different devices: /device:TPU:15 before, /device:TPU:0 now
where the time goes in v3:
time: 58 us; the launch traced here: 57.8 us
  Pallas kernels  54.2 us (93%)
  local copies, waits for them, and re-layouts  2.29 us (4%)
  between operations  1.3 us (2%)
    pallas_call x1, Pallas kernels, local(): pl.pallas_call(functools.partial(kernel, n), out_shape=jax.ShapeDtypeStru...  54.2 us
    unnamed x1, local copies, waits for them, and re-layouts  2.29 us

profile of v3, /device:TPU:0, one launch (start us, length us, event | category | flops | bytes accessed | tf_op | source)
XLA Modules:
  0.0 57.8 jit_solution(8990128759967551040)
XLA Ops:
  1.3 54.2 %shard_map.136 = bf16[128,4096]{1,0:T(8,128)(2,1)} custom-call(bf16[64,9216]{1,0:T(8,128)(2,1)} %xbc.1, bf16[64,8192]{1,0:T(8,128)(2,1)} %gate.1, bf16[64,128]{1,0:T(8,128)(2,1)} %dt.1, f32[4,9216]{1,0:T(4,128)} %weight.1, f32[1,9216]{1,0:T(1,128)} %bitcast.6, f32[1,64]{1,0:T(1,128)} %bitcast.8, f32[1,64]{1,0:T(1,128)} %bitcast.9, f32[64]{0:T(128)} %d_skip_h.1, ...), custom_call_target="tpu_custom_call" | custom-call | tf_op jit(solution)/shard_map/pallas_call | solution.py:422
  55.5 2.3 %copy.18 = bf16[128,4096]{1,0:T(8,128)(2,1)} copy(bf16[128,4096]{1,0:T(8,128)(2,1)} %shard_map.136) | data formatting | bytes 2097152
